TPU v7x, 128 devices: a whole 4x4x4 slice. The times are simulated.
128 devices in a mesh: frame: 8 (over x, core), cell: 16 (over y, z).
Axes of the slice: x: 4, y: 4, z: 4, core: 2. Of those that a mesh axis runs over, the one named last changes fastest.
Arguments:
- front: float32 [8, 4096, 4096], P('frame', 'cell')
- parent_of: int32 [8], replicated, may hold values from 0 to 7
- block_map: int32 [8, 13], replicated, may hold values from 3 to 31, as said below
- parent_in: bfloat16 [8, 2, 4096, 8192], P('frame', None, 'cell'), may hold values from -0.3125 to 0.3125
Outputs:
- lower_panel: float32 [8, 4096, 768], P('frame', 'cell')
- parent_out: bfloat16 [8, 2, 4096, 8192], P('frame', None, 'cell')
Inputs may be any that keep to these rules, and one draw needn't show every extreme that they name: block_map[c, k] is 3 + k or 3 + k + 16.
All inputs are finite; a program needn't handle non-finite values.
Results may differ from a plain program's by a relative error of at most 0.004.
Values may be sent and summed in bfloat16 or wider, within the bound.
A program may use at most 192 MiB of HBM per device.

v0:
```python
import jax
import jax.numpy as jnp
from jax import lax
from jax.sharding import PartitionSpec as P

PB = 3


def per_device(front, parent_of, block_map, parent_in):
    block_row = front[0]
    rows_here = block_row.shape[0]
    order = block_row.shape[1]
    blocks = order // rows_here
    width = PB * rows_here
    cell_index = lax.axis_index("cell")
    frame_index = lax.axis_index("frame")
    highest = lax.Precision.HIGHEST
    panel = lax.all_gather(block_row[:, :width], "cell", axis=0, tiled=True)
    l11 = jnp.linalg.cholesky(panel[:width])
    l21 = lax.linalg.triangular_solve(
        l11, panel[width:], left_side=False, lower=True, transpose_a=True
    )
    lower_all = jnp.concatenate([l11, l21], 0)
    my_lower = lax.dynamic_slice_in_dim(lower_all, cell_index * rows_here, rows_here, 0)
    product = jnp.dot(my_lower, l21.T, precision=highest)
    update = (block_row[:, width:] - product).astype(jnp.bfloat16)
    update_blocks = update.shape[1] // rows_here
    which_k = jnp.maximum(cell_index - PB, 0)
    whole_parent = parent_in[0].reshape(2, rows_here, 2, blocks, rows_here)
    region_start = whole_parent[:, :, :, PB:, :].astype(jnp.float32)
    pieces = lax.all_gather(update[None], "frame", axis=0, tiled=True)

    def one_child(step, acc):
        parent = lax.dynamic_index_in_dim(parent_of, step, 0, keepdims=False)
        positions = lax.dynamic_index_in_dim(block_map, step, 0, keepdims=False)
        target = lax.dynamic_index_in_dim(positions, which_k, 0, keepdims=False)
        live = (parent == frame_index) & (cell_index >= PB)
        half = target // blocks

        def add_piece(inner):
            piece = lax.dynamic_index_in_dim(pieces, step, 0, keepdims=False)
            piece = piece.reshape(rows_here, update_blocks, rows_here).astype(jnp.float32)
            upper = (positions >= blocks)[None, :, None]
            zeros = jnp.zeros_like(piece)
            delta = jnp.stack([jnp.where(upper, zeros, piece), jnp.where(upper, piece, zeros)], 1)
            current = lax.dynamic_index_in_dim(inner, half, 0, keepdims=False)
            return lax.dynamic_update_index_in_dim(inner, current + delta, half, 0)

        def keep_same(inner):
            return inner

        return lax.cond(live, add_piece, keep_same, acc)

    total = lax.fori_loop(0, pieces.shape[0], one_child, region_start)
    merged = jnp.concatenate([whole_parent[:, :, :, :PB, :], total.astype(jnp.bfloat16)], 3)
    merged = merged.reshape(2, rows_here, 2 * blocks * rows_here)
    return (my_lower[None], merged[None])


def solution(mesh):
    placed = (P("frame", "cell", None), P(), P(), P("frame", None, "cell", None))
    return jax.shard_map(
        per_device,
        mesh=mesh,
        in_specs=placed,
        out_specs=(P("frame", "cell", None), P("frame", None, "cell", None)),
        check_vma=False,
    )
```

profile of v0, /device:TPU:15, one launch (start us, length us, event | category | flops | bytes accessed | tf_op | source)
XLA Modules:
  0.0 594.5 jit_solution(12432647070224209038)
XLA Ops:
  7.2 5.6 copy.11
  15.0 101.0 %all-gather.4.cloned.1.call-done = f32[4096,768]{0,1:T(8,128)} async-done(((f32[256,768]{0,1:T(8,128)}), f32[4096,768]{0,1:T(8,128)}) %all-gather.4.cloned.1.call-update) | async-done | bytes 12582928 | tf_op jit(solution)/shard_map/all_gather | solution.py:18
  119.6 2.7 fusion.25
  123.7 11.7 %cholesky.165 = f32[128,128]{1,0:T(8,128)S(1)} custom-call(f32[128,128]{1,0:T(8,128)S(1)} %cholesky.424), custom_call_target="Cholesky" | custom-call | tf_op jit(solution)/shard_map/jit(cholesky)/cholesky | solution.py:19
  135.4 9.8 %custom-call.46 = f32[1,128,128]{1,2,0:T(8,128)S(1)} custom-call(f32[1,128,128]{2,1,0:T(8,128)S(1)} %get-tuple-element.497), custom_call_target="InvertDiagBlocksLowerTriangular" | custom-call | tf_op jit(solution)/shard_map/jit(cholesky)/cholesky | solution.py:19
  148.2 11.7 %cholesky.188 = f32[128,128]{1,0:T(8,128)S(1)} custom-call(f32[128,128]{1,0:T(8,128)S(1)} %cholesky.428), custom_call_target="Cholesky" | custom-call | tf_op jit(solution)/shard_map/jit(cholesky)/cholesky | solution.py:19
  160.0 10.1 %custom-call.47 = f32[1,128,128]{1,2,0:T(8,128)S(1)} custom-call(f32[1,128,128]{2,1,0:T(8,128)S(1)} %get-tuple-element.494), custom_call_target="InvertDiagBlocksLowerTriangular" | custom-call | tf_op jit(solution)/shard_map/jit(cholesky)/cholesky | solution.py:19
  172.0 11.7 %cholesky.354 = f32[128,128]{1,0:T(8,128)S(1)} custom-call(f32[128,128]{1,0:T(8,128)S(1)} %cholesky.433), custom_call_target="Cholesky" | custom-call | tf_op jit(solution)/shard_map/jit(cholesky)/cholesky | solution.py:19
  184.4 9.8 %custom-call.48 = f32[1,128,128]{1,2,0:T(8,128)S(1)} custom-call(f32[1,128,128]{2,1,0:T(8,128)S(1)} %get-tuple-element.491), custom_call_target="InvertDiagBlocksLowerTriangular" | custom-call | tf_op jit(solution)/shard_map/jit(cholesky)/cholesky | solution.py:19
  196.1 11.9 %cholesky.373 = f32[128,128]{1,0:T(8,128)S(1)} custom-call(f32[128,128]{1,0:T(8,128)S(1)} %cholesky.438), custom_call_target="Cholesky" | custom-call | tf_op jit(solution)/shard_map/jit(cholesky)/cholesky | solution.py:19
  208.7 9.8 %custom-call.49 = f32[1,128,128]{1,2,0:T(8,128)S(1)} custom-call(f32[1,128,128]{2,1,0:T(8,128)S(1)} %get-tuple-element.488), custom_call_target="InvertDiagBlocksLowerTriangular" | custom-call | tf_op jit(solution)/shard_map/jit(cholesky)/cholesky | solution.py:19
  220.3 11.7 %cholesky.392 = f32[128,128]{1,0:T(8,128)S(1)} custom-call(f32[128,128]{1,0:T(8,128)S(1)} %cholesky.443), custom_call_target="Cholesky" | custom-call | tf_op jit(solution)/shard_map/jit(cholesky)/cholesky | solution.py:19
  232.7 9.8 %custom-call.50 = f32[1,128,128]{1,2,0:T(8,128)S(1)} custom-call(f32[1,128,128]{2,1,0:T(8,128)S(1)} %get-tuple-element.485), custom_call_target="InvertDiagBlocksLowerTriangular" | custom-call | tf_op jit(solution)/shard_map/jit(cholesky)/cholesky | solution.py:19
  244.0 12.1 %cholesky.410 = f32[128,128]{1,0:T(8,128)S(1)} custom-call(f32[128,128]{1,0:T(8,128)S(1)} %convolution_subtract_fusion.8), custom_call_target="Cholesky" | custom-call | tf_op jit(solution)/shard_map/jit(cholesky)/cholesky | solution.py:19
  261.1 2.5 fusion.26
  263.5 17.4 %while.21 = (s32[]{:T(128)}, f32[768,768]{1,0:T(8,128)}, s32[6,2]{0,1:T(2,128)S(1)}, f32[6,128,128]{2,1,0:T(8,128)S(1)}, s32[]{:T(128)}) while((s32[]{:T(128)}, f32[768,768]{1,0:T(8,128)}, s32[6,2]{0,1:T(2,128)S(1)}, f32[6,128,128]{2,1,0:T(8,128)S(1)}, s32[]{:T(128)}) %tuple.115), condition=%wide.while_cond, body=%wide.while_body.sunk | while | flops 2 | bytes 131181 | solution.py:20
  264.2 2.3 bitcast_dynamic-update-slice_fusion.2
  267.1 2.3 bitcast_dynamic-update-slice_fusion.2
  270.0 2.3 bitcast_dynamic-update-slice_fusion.2
  272.9 2.3 bitcast_dynamic-update-slice_fusion.2
  275.8 2.3 bitcast_dynamic-update-slice_fusion.2
  281.0 59.0 %custom-call.51 = f32[6,128,128]{1,2,0:T(8,128)S(1)} custom-call(f32[6,128,128]{2,1,0:T(8,128)S(1)} %get-tuple-element.425), custom_call_target="InvertDiagBlocksLowerTriangular" | custom-call | tf_op jit(solution)/shard_map/triangular_solve | solution.py:20
  342.1 3.1 constant_dynamic-update-slice_fusion.4
  345.2 3.3 convolution_subtract_fusion.3
  350.3 3.8 convolution_subtract_fusion.2
  354.0 2.6 constant_dynamic-update-slice_fusion.2
  356.6 3.2 copy-done.1
  359.9 4.9 fusion.16
  364.8 4.3 constant_dynamic-update-slice_fusion.1
  369.2 7.1 %fusion.19 = f32[3328,128]{0,1:T(8,128)} fusion(f32[3328,128]{0,1:T(8,128)} %get-tuple-element.503, f32[3328,128]{0,1:T(8,128)} %copy-done.2, f32[3328,128]{0,1:T(8,128)S(1)} %get-tuple-element.501, f32[3328,128]{0,1:T(8,128)S(1)} %bitcast.107, f32[4096,768]{0,1:T(8,128)S(1)} %bitcast.111, f32[768,768]{1,0:T(8,128)} %get-tuple-element.639), kind=kOutput, calls=%fused_computation.35 | convolution fusion | flops 2622783488 | bytes 10485760 | tf_op jit(solution)/shard_map/triangular_solve | solution.py:20
  376.3 4.3 constant_dynamic-update-slice_fusion
  380.6 8.5 %convolution_subtract_fusion.1 = f32[3328,128]{0,1:T(8,128)S(1)} fusion(f32[3328,640]{0,1:T(8,128)} %get-tuple-element.472, f32[4096,768]{0,1:T(8,128)S(1)} %bitcast.111, f32[768,768]{1,0:T(8,128)} %get-tuple-element.639), kind=kOutput, calls=%fused_computation.31 | convolution fusion | flops 3271983104 | bytes 12255232 | tf_op jit(solution)/shard_map/triangular_solve | solution.py:20
  389.1 2.5 convolution_dynamic-update-slice_fusion
  393.8 18.2 %fusion.9 = bf16[256,3328]{0,1:T(8,128)(2,1)} fusion(f32[256,768]{0,1:T(8,128)S(1)} %fusion.29, f32[3328,768]{0,1:T(8,128)S(1)} %convolution_dynamic-update-slice_fusion, f32[256,4096]{0,1:T(8,128)S(1)} %bitcast.109), kind=kOutput, calls=%fused_computation.24 | convolution fusion | flops 7853441024 | bytes 16121856 | tf_op jit(solution)/shard_map/dot_general | solution.py:25
  412.0 12.0 %copy.15 = bf16[1,2,256,8192]{2,3,1,0:T(8,128)(2,1)} copy(bf16[1,2,256,8192]{3,2,1,0:T(8,128)(2,1)} %param.11) | data formatting | bytes 16777216 | tf_op args[3]
  425.7 9.8 %slice_convert_fusion = f32[2,256,2,13,256]{1,4,3,2,0:T(8,128)} fusion(bf16[2,256,2,16,256]{1,4,3,2,0:T(8,128)(2,1)} %bitcast.103), kind=kLoop, calls=%fused_computation.13 | loop fusion | flops 3407872 | bytes 20447232 | tf_op jit(solution)/shard_map/convert_element_type | solution.py:30
  436.7 52.1 %all-gather.6.cloned.1.call-done = bf16[2048,3328]{0,1:T(8,128)(2,1)} async-done(((bf16[256,3328]{0,1:T(8,128)(2,1)}), bf16[2048,3328]{0,1:T(8,128)(2,1)}) %all-gather.6.cloned.1.call-update) | async-done | bytes 13631504 | tf_op jit(solution)/shard_map/all_gather | solution.py:31
  488.8 12.5 %copy.23 = bf16[416,8,8,256]{3,2,0,1:T(8,128)(2,1)} copy(bf16[416,8,8,256]{3,2,1,0:T(8,128)(2,1)} %bitcast.112) | data formatting | bytes 27262976 | tf_op jit(solution)/shard_map/all_gather | solution.py:31
  501.3 58.4 %while.20 = (s32[]{:T(128)}, f32[2,256,2,13,256]{1,4,3,2,0:T(8,128)}, s32[8]{0:T(128)S(1)}, s32[]{:T(128)}, pred[]{:T(512)}, /*index=5*/s32[8,13]{1,0:T(8,128)},...) while((s32[]{:T(128)}, f32[2,256,2,13,256]{1,4,3,2,0:T(8,128)}, ...), condition=%wide.region_15.16_spmd, body=%wide.region_12.15_spmd.sunk | while | flops 5963816 | bytes 32375320 | solution.py:54
  504.1 12.4 %conditional.2 = (f32[2,256,2,13,256]{1,4,3,2,0:T(8,128)}) conditional(s32[]{:T(128)} %convert_element_type.50, f32[2,256,2,13,256]{1,4,3,2,0:T(8,128)} %get-tuple-element.611, (s32[]{:T(128)}, s32[]{:T(128)}, f32[2,256,2,13,256]{1,4,3,2,0:T(8,128)}, s32[8,13]{1,0:T(8,128)}, s32[]{:T(128)}, /*index=5*/bf16[8,256,3328]{1,2,0:T(8,128)(2,1)}, ...), branch_computations={%region_13.13_spmd, %region_14.14_spmd} | conditional | flops 5963810 | bytes 32375100 | solution.py:52
  509.9 6.6 %fusion = f32[2,256,2,13,256]{1,4,3,2,0:T(8,128)} fusion(f32[2,256,2,13,256]{1,4,3,2,0:T(8,128)} %get-tuple-element.397, s32[]{:T(128)S(6)} %select_n.87, f32[1,256,1,13,256]{1,4,3,2,0:T(8,128)S(1)} %get-tuple-element.469, f32[1,256,1,13,256]{1,4,3,2,0:T(8,128)S(1)} %get-tuple-element.468), kind=kLoop, calls=%fused_computation.1 | loop fusion | flops 3407872 | bytes 20447236 | tf_op jit(solution)/shard_map/while/body/eval_jaxpr/cond/branch_1_fun/jit(dynamic_update_index_in_dim)/dynamic_update_slice | solution.py:47
  527.0 12.5 %conditional.2 = (f32[2,256,2,13,256]{1,4,3,2,0:T(8,128)}) conditional(s32[]{:T(128)} %convert_element_type.50, f32[2,256,2,13,256]{1,4,3,2,0:T(8,128)} %get-tuple-element.611, (s32[]{:T(128)}, s32[]{:T(128)}, f32[2,256,2,13,256]{1,4,3,2,0:T(8,128)}, s32[8,13]{1,0:T(8,128)}, s32[]{:T(128)}, /*index=5*/bf16[8,256,3328]{1,2,0:T(8,128)(2,1)}, ...), branch_computations={%region_13.13_spmd, %region_14.14_spmd} | conditional | flops 5963810 | bytes 32375100 | solution.py:52
  532.8 6.6 %fusion = f32[2,256,2,13,256]{1,4,3,2,0:T(8,128)} fusion(f32[2,256,2,13,256]{1,4,3,2,0:T(8,128)} %get-tuple-element.397, s32[]{:T(128)S(6)} %select_n.87, f32[1,256,1,13,256]{1,4,3,2,0:T(8,128)S(1)} %get-tuple-element.469, f32[1,256,1,13,256]{1,4,3,2,0:T(8,128)S(1)} %get-tuple-element.468), kind=kLoop, calls=%fused_computation.1 | loop fusion | flops 3407872 | bytes 20447236 | tf_op jit(solution)/shard_map/while/body/eval_jaxpr/cond/branch_1_fun/jit(dynamic_update_index_in_dim)/dynamic_update_slice | solution.py:47
  542.0 12.4 %conditional.2 = (f32[2,256,2,13,256]{1,4,3,2,0:T(8,128)}) conditional(s32[]{:T(128)} %convert_element_type.50, f32[2,256,2,13,256]{1,4,3,2,0:T(8,128)} %get-tuple-element.611, (s32[]{:T(128)}, s32[]{:T(128)}, f32[2,256,2,13,256]{1,4,3,2,0:T(8,128)}, s32[8,13]{1,0:T(8,128)}, s32[]{:T(128)}, /*index=5*/bf16[8,256,3328]{1,2,0:T(8,128)(2,1)}, ...), branch_computations={%region_13.13_spmd, %region_14.14_spmd} | conditional | flops 5963810 | bytes 32375100 | solution.py:52
  547.8 6.6 %fusion = f32[2,256,2,13,256]{1,4,3,2,0:T(8,128)} fusion(f32[2,256,2,13,256]{1,4,3,2,0:T(8,128)} %get-tuple-element.397, s32[]{:T(128)S(6)} %select_n.87, f32[1,256,1,13,256]{1,4,3,2,0:T(8,128)S(1)} %get-tuple-element.469, f32[1,256,1,13,256]{1,4,3,2,0:T(8,128)S(1)} %get-tuple-element.468), kind=kLoop, calls=%fused_computation.1 | loop fusion | flops 3407872 | bytes 20447236 | tf_op jit(solution)/shard_map/while/body/eval_jaxpr/cond/branch_1_fun/jit(dynamic_update_index_in_dim)/dynamic_update_slice | solution.py:47
  559.6 8.7 %convert_element_type.45 = bf16[2,256,2,13,256]{1,4,3,2,0:T(8,128)(2,1)} convert(f32[2,256,2,13,256]{1,4,3,2,0:T(8,128)} %get-tuple-element.415) | non-fusion elementwise | flops 3407872 | bytes 20447232 | tf_op jit(solution)/shard_map/convert_element_type | solution.py:55
  568.4 6.9 %pad_maximum_fusion = bf16[2,256,2,16,256]{1,4,3,2,0:T(8,128)(2,1)} fusion(bf16[2,256,2,13,256]{1,4,3,2,0:T(8,128)(2,1)} %convert_element_type.45, bf16[2,256,2,3,256]{1,4,3,2,0:T(8,128)(2,1)S(1)} %slice.203), kind=kLoop, calls=%fused_computation.12 | loop fusion | flops 4194304 | bytes 16777216 | tf_op jit(solution)/shard_map/concatenate | solution.py:55
  575.2 12.0 %copy.20 = bf16[1,2,256,8192]{3,2,1,0:T(8,128)(2,1)} copy(bf16[1,2,256,8192]{2,3,1,0:T(8,128)(2,1)} %bitcast.104) | data formatting | bytes 16777216 | tf_op jit(solution)/shard_map/broadcast_in_dim;reshape | solution.py:57
  (104 shorter events, 60.4 us)
Async XLA Ops:
  7.2 108.8 %all-gather.4.cloned.1.call-start = ((), (), s32[]{:S(2)}) async-start(), calls=%async_computation | async-start | bytes 13369344 | tf_op jit(solution)/shard_map/all_gather | solution.py:18
  14.9 473.9 %all-gather.6.cloned.1.call-start = ((), (), s32[]{:S(2)}) async-start(), calls=%async_computation.1 | async-start | bytes 15335424 | tf_op jit(solution)/shard_map/all_gather | solution.py:31
  115.9 1.7 slice-start.3
  122.3 1.4 copy-start.3
  339.9 8.6 %copy-start.4 = (f32[6,128,128]{1,2,0:T(8,128)}, f32[6,128,128]{1,2,0:T(8,128)S(1)}, u32[]{:S(2)}) copy-start(f32[6,128,128]{1,2,0:T(8,128)S(1)} %custom-call.51) | copy-start | bytes 1179652
  345.2 14.6 %slice-start = ((s8[12582912]{0:T(1024)(128)(4,1)}), s8[4194304]{0:T(1024)(128)(4,1)S(1)}, s32[]{:S(2)}) async-start(s8[12582912]{0:T(1024)(128)(4,1)} %bitcast.110), calls=%async_computation.2 | async-start | bytes 8388608
  348.5 11.3 %slice-start.1 = ((s8[12582912]{0:T(1024)(128)(4,1)}), s8[4194304]{0:T(1024)(128)(4,1)S(1)}, s32[]{:S(2)}) async-start(s8[12582912]{0:T(1024)(128)(4,1)} %bitcast.110), calls=%async_computation.3 | async-start | bytes 8388608
  350.3 9.6 %slice-start.2 = ((s8[12582912]{0:T(1024)(128)(4,1)}), s8[4194304]{0:T(1024)(128)(4,1)S(1)}, s32[]{:S(2)}) async-start(s8[12582912]{0:T(1024)(128)(4,1)} %bitcast.110), calls=%async_computation.4 | async-start | bytes 8388608
  356.6 3.2 copy-start.1
  359.9 5.0 copy-start.2
  391.6 2.2 copy-start
  488.8 12.5 %copy-start.5 = (s32[8]{0:T(128)S(1)}, s32[8]{0:T(128)}, u32[]{:S(2)}) copy-start(s32[8]{0:T(128)} %param.9) | copy-start | bytes 100
Sparse Core Ops, SparseCore 0:
  15.0 100.8 all-gather.3
  412.1 76.6 all-gather.5
where the time goes:
time: 606 us; the launch traced here: 594 us
  other arithmetic  238 us (39%)
  waiting for transfers between devices  153 us (25%)
  local copies, waits for them, and re-layouts  97.1 us (16%)
  matrix products  74 us (12%)
  between operations  18.5 us (3%)
  loops' own time  14 us (2%)
    another operation x22, other arithmetic, per_device(): l11 = jnp.linalg.cholesky(panel[:width])  124 us
    all_gather x1, waiting for transfers between devices, per_device(): panel = lax.all_gather(block_row[:, :width], 'cell', axis=0, tiled=True)  101 us
    another operation x3, other arithmetic, per_device(): lax.linalg.triangular_solve(l11, panel[width:], left_side=False, lower=Tr...  61.4 us
    all_gather x1, waiting for transfers between devices, per_device(): pieces = lax.all_gather(update[None], 'frame', axis=0, tiled=True)  52.1 us
    another operation x11, matrix products, per_device(): lax.linalg.triangular_solve(l11, panel[width:], left_side=False, lower=Tr...  46.1 us
    unnamed x20, local copies, waits for them, and re-layouts  24.3 us
    dynamic_update_slice x3, other arithmetic, add_piece(): return lax.dynamic_update_index_in_dim(inner, current + delta, half, 0)  19.8 us
    dot_general x1, matrix products, per_device(): product = jnp.dot(my_lower, l21.T, precision=highest)  18.2 us
  transfers between devices with their start and end apart: 2, of which 2 were waited for; matrix products, arithmetic and copies ran while one was open for 4% of the time, Pallas kernels for 0%

commit v1 on v0

--- a/solution.py
+++ b/solution.py
@@ -28,7 +28,9 @@
     which_k = jnp.maximum(cell_index - PB, 0)
     whole_parent = parent_in[0].reshape(2, rows_here, 2, blocks, rows_here)
     region_start = whole_parent[:, :, :, PB:, :].astype(jnp.float32)
-    pieces = lax.all_gather(update[None], "frame", axis=0, tiled=True)
+    part = update[None]
+    sent = jnp.stack([part] * lax.axis_size("frame"))
+    pieces = jnp.concatenate(lax.all_to_all(sent, "frame", 0, 0), axis=0)
 
     def one_child(step, acc):
         parent = lax.dynamic_index_in_dim(parent_of, step, 0, keepdims=False)

time: 606 us -> 676 us (1.12)
  waiting for transfers between devices: 153 us -> 225 us
  starting transfers between devices: 0.08 us -> 7.47 us
  local copies, waits for them, and re-layouts: 97.1 us -> 90 us
    all_to_all x0 -> x1, waiting for transfers between devices: none -> 124 us  [per_device(): pieces = jnp.concatenate(lax.all_to_all(sent, 'frame', 0, 0), axis=0)]
    all_gather x1 -> x0, waiting for transfers between devices: 52.1 us -> none  [per_device(): pieces = lax.all_gather(update[None], 'frame', axis=0, tiled=True)]
    all_gather x1 -> x0, local copies, waits for them, and re-layouts: 12.5 us -> none  [per_device(): pieces = lax.all_gather(update[None], 'frame', axis=0, tiled=True)]
    all_to_all x0 -> x1, starting transfers between devices: none -> 7.43 us  [per_device(): pieces = jnp.concatenate(lax.all_to_all(sent, 'frame', 0, 0), axis=0)]
    another operation x18 -> x19, local copies, waits for them, and re-layouts: 17.3 us -> 23.8 us
where the time goes in v1:
time: 676 us; the launch traced here: 664 us
  other arithmetic  238 us (35%)
  waiting for transfers between devices  225 us (33%)
  local copies, waits for them, and re-layouts  90 us (13%)
  matrix products  73.4 us (11%)
  between operations  18.7 us (3%)
  loops' own time  12.2 us (2%)
  starting transfers between devices  7.47 us (1%)
    all_to_all x1, waiting for transfers between devices, per_device(): pieces = jnp.concatenate(lax.all_to_all(sent, 'frame', 0, 0), axis=0)  124 us
    another operation x22, other arithmetic, per_device(): l11 = jnp.linalg.cholesky(panel[:width])  124 us
    all_gather x1, waiting for transfers between devices, per_device(): panel = lax.all_gather(block_row[:, :width], 'cell', axis=0, tiled=True)  101 us
    another operation x3, other arithmetic, per_device(): lax.linalg.triangular_solve(l11, panel[width:], left_side=False, lower=Tr...  61.4 us
    another operation x11, matrix products, per_device(): lax.linalg.triangular_solve(l11, panel[width:], left_side=False, lower=Tr...  46.1 us
    unnamed x20, local copies, waits for them, and re-layouts  24.2 us
    dynamic_update_slice x3, other arithmetic, add_piece(): return lax.dynamic_update_index_in_dim(inner, current + delta, half, 0)  19.8 us
    another operation x18, local copies, waits for them, and re-layouts  18 us
  transfers between devices with their start and end apart: 2, of which 2 were waited for; matrix products, arithmetic and copies ran while one was open for 4% of the time, Pallas kernels for 0%

profile of v1, /device:TPU:15, one launch (start us, length us, event | category | flops | bytes accessed | tf_op | source)
XLA Modules:
  0.0 664.4 jit_solution(3741607135633893238)
XLA Ops:
  7.2 5.6 copy.18
  14.9 101.0 %all-gather.2.cloned.1.call-done = f32[4096,768]{0,1:T(8,128)} async-done(((f32[256,768]{0,1:T(8,128)}), f32[4096,768]{0,1:T(8,128)}) %all-gather.2.cloned.1.call-update) | async-done | bytes 12582928 | tf_op jit(solution)/shard_map/all_gather | solution.py:18
  119.6 2.7 fusion.25
  123.7 11.7 %cholesky.165 = f32[128,128]{1,0:T(8,128)S(1)} custom-call(f32[128,128]{1,0:T(8,128)S(1)} %cholesky.424), custom_call_target="Cholesky" | custom-call | tf_op jit(solution)/shard_map/jit(cholesky)/cholesky | solution.py:19
  135.4 9.8 %custom-call.46 = f32[1,128,128]{1,2,0:T(8,128)S(1)} custom-call(f32[1,128,128]{2,1,0:T(8,128)S(1)} %get-tuple-element.481), custom_call_target="InvertDiagBlocksLowerTriangular" | custom-call | tf_op jit(solution)/shard_map/jit(cholesky)/cholesky | solution.py:19
  148.2 11.7 %cholesky.188 = f32[128,128]{1,0:T(8,128)S(1)} custom-call(f32[128,128]{1,0:T(8,128)S(1)} %cholesky.428), custom_call_target="Cholesky" | custom-call | tf_op jit(solution)/shard_map/jit(cholesky)/cholesky | solution.py:19
  160.0 10.1 %custom-call.47 = f32[1,128,128]{1,2,0:T(8,128)S(1)} custom-call(f32[1,128,128]{2,1,0:T(8,128)S(1)} %get-tuple-element.478), custom_call_target="InvertDiagBlocksLowerTriangular" | custom-call | tf_op jit(solution)/shard_map/jit(cholesky)/cholesky | solution.py:19
  172.0 11.7 %cholesky.354 = f32[128,128]{1,0:T(8,128)S(1)} custom-call(f32[128,128]{1,0:T(8,128)S(1)} %cholesky.433), custom_call_target="Cholesky" | custom-call | tf_op jit(solution)/shard_map/jit(cholesky)/cholesky | solution.py:19
  184.5 9.8 %custom-call.48 = f32[1,128,128]{1,2,0:T(8,128)S(1)} custom-call(f32[1,128,128]{2,1,0:T(8,128)S(1)} %get-tuple-element.475), custom_call_target="InvertDiagBlocksLowerTriangular" | custom-call | tf_op jit(solution)/shard_map/jit(cholesky)/cholesky | solution.py:19
  196.2 11.9 %cholesky.373 = f32[128,128]{1,0:T(8,128)S(1)} custom-call(f32[128,128]{1,0:T(8,128)S(1)} %cholesky.438), custom_call_target="Cholesky" | custom-call | tf_op jit(solution)/shard_map/jit(cholesky)/cholesky | solution.py:19
  208.8 9.8 %custom-call.49 = f32[1,128,128]{1,2,0:T(8,128)S(1)} custom-call(f32[1,128,128]{2,1,0:T(8,128)S(1)} %get-tuple-element.472), custom_call_target="InvertDiagBlocksLowerTriangular" | custom-call | tf_op jit(solution)/shard_map/jit(cholesky)/cholesky | solution.py:19
  220.4 11.7 %cholesky.392 = f32[128,128]{1,0:T(8,128)S(1)} custom-call(f32[128,128]{1,0:T(8,128)S(1)} %cholesky.443), custom_call_target="Cholesky" | custom-call | tf_op jit(solution)/shard_map/jit(cholesky)/cholesky | solution.py:19
  232.7 9.8 %custom-call.50 = f32[1,128,128]{1,2,0:T(8,128)S(1)} custom-call(f32[1,128,128]{2,1,0:T(8,128)S(1)} %get-tuple-element.469), custom_call_target="InvertDiagBlocksLowerTriangular" | custom-call | tf_op jit(solution)/shard_map/jit(cholesky)/cholesky | solution.py:19
  244.1 12.1 %cholesky.410 = f32[128,128]{1,0:T(8,128)S(1)} custom-call(f32[128,128]{1,0:T(8,128)S(1)} %convolution_subtract_fusion.8), custom_call_target="Cholesky" | custom-call | tf_op jit(solution)/shard_map/jit(cholesky)/cholesky | solution.py:19
  261.3 2.5 fusion.26
  263.8 18.1 %while.21 = (s32[]{:T(128)}, f32[768,768]{1,0:T(8,128)}, s32[6,2]{0,1:T(2,128)S(1)}, f32[6,128,128]{2,1,0:T(8,128)S(1)}, s32[]{:T(128)}) while((s32[]{:T(128)}, f32[768,768]{1,0:T(8,128)}, s32[6,2]{0,1:T(2,128)S(1)}, f32[6,128,128]{2,1,0:T(8,128)S(1)}, s32[]{:T(128)}) %tuple.113), condition=%wide.while_cond, body=%wide.while_body.sunk | while | flops 2 | bytes 131181 | solution.py:20
  264.5 2.3 bitcast_dynamic-update-slice_fusion.2
  267.5 2.3 bitcast_dynamic-update-slice_fusion.2
  270.5 2.3 bitcast_dynamic-update-slice_fusion.2
  273.6 2.3 bitcast_dynamic-update-slice_fusion.2
  281.9 59.0 %custom-call.51 = f32[6,128,128]{1,2,0:T(8,128)S(1)} custom-call(f32[6,128,128]{2,1,0:T(8,128)S(1)} %get-tuple-element.425), custom_call_target="InvertDiagBlocksLowerTriangular" | custom-call | tf_op jit(solution)/shard_map/triangular_solve | solution.py:20
  343.1 3.1 constant_dynamic-update-slice_fusion.4
  346.2 3.3 convolution_subtract_fusion.3
  351.2 3.8 convolution_subtract_fusion.2
  355.0 2.6 constant_dynamic-update-slice_fusion.2
  357.6 3.2 copy-done.1
  360.8 4.9 fusion.16
  365.8 4.4 constant_dynamic-update-slice_fusion.1
  370.1 7.1 %fusion.19 = f32[3328,128]{0,1:T(8,128)} fusion(f32[3328,128]{0,1:T(8,128)} %get-tuple-element.487, f32[3328,128]{0,1:T(8,128)} %copy-done.2, f32[3328,128]{0,1:T(8,128)S(1)} %get-tuple-element.485, f32[3328,128]{0,1:T(8,128)S(1)} %bitcast.103, f32[4096,768]{0,1:T(8,128)S(1)} %bitcast.107, f32[768,768]{1,0:T(8,128)} %get-tuple-element.621), kind=kOutput, calls=%fused_computation.34 | convolution fusion | flops 2622783488 | bytes 10485760 | tf_op jit(solution)/shard_map/triangular_solve | solution.py:20
  377.3 4.3 constant_dynamic-update-slice_fusion
  381.5 8.5 %convolution_subtract_fusion.1 = f32[3328,128]{0,1:T(8,128)S(1)} fusion(f32[3328,640]{0,1:T(8,128)} %get-tuple-element.456, f32[4096,768]{0,1:T(8,128)S(1)} %bitcast.107, f32[768,768]{1,0:T(8,128)} %get-tuple-element.621), kind=kOutput, calls=%fused_computation.30 | convolution fusion | flops 3271983104 | bytes 12255232 | tf_op jit(solution)/shard_map/triangular_solve | solution.py:20
  390.0 2.5 convolution_dynamic-update-slice_fusion
  394.7 17.5 %fusion.9 = bf16[256,3328]{0,1:T(8,128)(2,1)S(1)} fusion(f32[256,768]{0,1:T(8,128)S(1)} %fusion.29, f32[3328,768]{0,1:T(8,128)S(1)} %convolution_dynamic-update-slice_fusion, f32[256,4096]{0,1:T(8,128)S(1)} %bitcast.105), kind=kOutput, calls=%fused_computation.23 | convolution fusion | flops 7853441024 | bytes 16121856 | tf_op jit(solution)/shard_map/dot_general | solution.py:25
  412.2 5.8 stack.8
  418.0 7.4 %all-to-all-start = ((bf16[8,1,256,3328]{2,3,1,0:T(8,128)(2,1)}), bf16[8,1,256,3328]{2,3,1,0:T(8,128)(2,1)}, u32[]{:S(2)}, u32[]{:S(2)}) async-start(bf16[8,1,256,3328]{2,3,1,0:T(8,128)(2,1)} %stack.8), calls=%async_computation | async-start | bytes 27262976 | tf_op jit(solution)/shard_map/all_to_all | solution.py:33
  425.5 11.9 %copy.27 = bf16[1,2,256,8192]{2,3,1,0:T(8,128)(2,1)} copy(bf16[1,2,256,8192]{3,2,1,0:T(8,128)(2,1)} %param.11) | data formatting | bytes 16777216 | tf_op args[3]
  438.9 9.5 %slice_convert_fusion = f32[2,256,2,13,256]{1,4,3,2,0:T(8,128)} fusion(bf16[2,256,2,16,256]{1,4,3,2,0:T(8,128)(2,1)} %bitcast.99), kind=kLoop, calls=%fused_computation.12 | loop fusion | flops 3407872 | bytes 20447232 | tf_op jit(solution)/shard_map/convert_element_type | solution.py:30
  449.6 124.1 %all-to-all-done = bf16[8,1,256,3328]{2,3,1,0:T(8,128)(2,1)} async-done(((bf16[8,1,256,3328]{2,3,1,0:T(8,128)(2,1)}), bf16[8,1,256,3328]{2,3,1,0:T(8,128)(2,1)}, u32[]{:S(2)}, u32[]{:S(2)}) %all-to-all-start) | async-done | bytes 13631520 | tf_op jit(solution)/shard_map/all_to_all | solution.py:33
  573.7 55.8 %while.20 = (s32[]{:T(128)}, f32[2,256,2,13,256]{1,4,3,2,0:T(8,128)}, s32[8]{0:T(128)S(1)}, s32[]{:T(128)}, pred[]{:T(512)}, /*index=5*/s32[8,13]{1,0:T(8,128)},...) while((s32[]{:T(128)}, f32[2,256,2,13,256]{1,4,3,2,0:T(8,128)}, ...), condition=%wide.region_15.16_spmd, body=%wide.region_12.15_spmd.sunk | while | flops 5963816 | bytes 32375320 | solution.py:56
  576.2 11.9 %conditional.2 = (f32[2,256,2,13,256]{1,4,3,2,0:T(8,128)}) conditional(s32[]{:T(128)} %convert_element_type.50, f32[2,256,2,13,256]{1,4,3,2,0:T(8,128)} %get-tuple-element.595, (s32[]{:T(128)}, s32[]{:T(128)}, f32[2,256,2,13,256]{1,4,3,2,0:T(8,128)}, s32[8,13]{1,0:T(8,128)}, s32[]{:T(128)}, /*index=5*/bf16[8,256,3328]{1,2,0:T(8,128)(2,1)}, ...), branch_computations={%region_13.13_spmd, %region_14.14_spmd} | conditional | flops 5963810 | bytes 32375100 | solution.py:54
  581.5 6.6 fusion
  598.2 11.9 %conditional.2 = (f32[2,256,2,13,256]{1,4,3,2,0:T(8,128)}) conditional(s32[]{:T(128)} %convert_element_type.50, f32[2,256,2,13,256]{1,4,3,2,0:T(8,128)} %get-tuple-element.595, (s32[]{:T(128)}, s32[]{:T(128)}, f32[2,256,2,13,256]{1,4,3,2,0:T(8,128)}, s32[8,13]{1,0:T(8,128)}, s32[]{:T(128)}, /*index=5*/bf16[8,256,3328]{1,2,0:T(8,128)(2,1)}, ...), branch_computations={%region_13.13_spmd, %region_14.14_spmd} | conditional | flops 5963810 | bytes 32375100 | solution.py:54
  603.5 6.6 fusion
  612.6 11.9 %conditional.2 = (f32[2,256,2,13,256]{1,4,3,2,0:T(8,128)}) conditional(s32[]{:T(128)} %convert_element_type.50, f32[2,256,2,13,256]{1,4,3,2,0:T(8,128)} %get-tuple-element.595, (s32[]{:T(128)}, s32[]{:T(128)}, f32[2,256,2,13,256]{1,4,3,2,0:T(8,128)}, s32[8,13]{1,0:T(8,128)}, s32[]{:T(128)}, /*index=5*/bf16[8,256,3328]{1,2,0:T(8,128)(2,1)}, ...), branch_computations={%region_13.13_spmd, %region_14.14_spmd} | conditional | flops 5963810 | bytes 32375100 | solution.py:54
  617.9 6.6 fusion
  629.6 8.7 %convert_element_type.45 = bf16[2,256,2,13,256]{1,4,3,2,0:T(8,128)(2,1)} convert(f32[2,256,2,13,256]{1,4,3,2,0:T(8,128)} %get-tuple-element.415) | non-fusion elementwise | flops 3407872 | bytes 20447232 | tf_op jit(solution)/shard_map/convert_element_type | solution.py:57
  638.3 6.9 %pad_maximum_fusion = bf16[2,256,2,16,256]{1,4,3,2,0:T(8,128)(2,1)} fusion(bf16[2,256,2,13,256]{1,4,3,2,0:T(8,128)(2,1)} %convert_element_type.45, bf16[2,256,2,3,256]{1,4,3,2,0:T(8,128)(2,1)S(1)} %slice.203), kind=kLoop, calls=%fused_computation.11 | loop fusion | flops 4194304 | bytes 16777216 | tf_op jit(solution)/shard_map/concatenate | solution.py:57
  645.1 12.0 %copy.36 = bf16[1,2,256,8192]{3,2,1,0:T(8,128)(2,1)} copy(bf16[1,2,256,8192]{2,3,1,0:T(8,128)(2,1)} %bitcast.100) | data formatting | bytes 16777216 | tf_op jit(solution)/shard_map/broadcast_in_dim;reshape | solution.py:59
  (103 shorter events, 62.1 us)
Async XLA Ops:
  7.2 108.8 %all-gather.2.cloned.1.call-start = ((), (), s32[]{:S(2)}) async-start(), calls=%async_computation.1 | async-start | bytes 13369344 | tf_op jit(solution)/shard_map/all_gather | solution.py:18
  115.9 1.7 slice-start.3
  122.3 1.4 copy-start.3
  340.9 8.6 %copy-start.4 = (f32[6,128,128]{1,2,0:T(8,128)}, f32[6,128,128]{1,2,0:T(8,128)S(1)}, u32[]{:S(2)}) copy-start(f32[6,128,128]{1,2,0:T(8,128)S(1)} %custom-call.51) | copy-start | bytes 1179652
  346.2 14.6 %slice-start = ((s8[12582912]{0:T(1024)(128)(4,1)}), s8[4194304]{0:T(1024)(128)(4,1)S(1)}, s32[]{:S(2)}) async-start(s8[12582912]{0:T(1024)(128)(4,1)} %bitcast.106), calls=%async_computation.2 | async-start | bytes 8388608
  349.5 11.3 %slice-start.1 = ((s8[12582912]{0:T(1024)(128)(4,1)}), s8[4194304]{0:T(1024)(128)(4,1)S(1)}, s32[]{:S(2)}) async-start(s8[12582912]{0:T(1024)(128)(4,1)} %bitcast.106), calls=%async_computation.3 | async-start | bytes 8388608
  351.2 9.6 %slice-start.2 = ((s8[12582912]{0:T(1024)(128)(4,1)}), s8[4194304]{0:T(1024)(128)(4,1)S(1)}, s32[]{:S(2)}) async-start(s8[12582912]{0:T(1024)(128)(4,1)} %bitcast.106), calls=%async_computation.4 | async-start | bytes 8388608
  357.5 3.2 copy-start.1
  360.8 5.0 copy-start.2
  392.5 2.2 copy-start
  418.0 155.7 %all-to-all-start = ((bf16[8,1,256,3328]{2,3,1,0:T(8,128)(2,1)}), bf16[8,1,256,3328]{2,3,1,0:T(8,128)(2,1)}, u32[]{:S(2)}, u32[]{:S(2)}) async-start(bf16[8,1,256,3328]{2,3,1,0:T(8,128)(2,1)} %stack.8), calls=%async_computation | async-start | bytes 27262976 | tf_op jit(solution)/shard_map/all_to_all | solution.py:33
  438.9 134.8 %copy-start.5 = (s32[8]{0:T(128)S(1)}, s32[8]{0:T(128)}, u32[]{:S(2)}) copy-start(s32[8]{0:T(128)} %param.9) | copy-start | bytes 100
Sparse Core Ops, SparseCore 0:
  15.0 100.8 all-gather.1
